TPU v7x, 256 devices: a whole 4x4x8 slice. The times are simulated.
256 devices in a mesh: atom: 16 (over z_hi, x, core), row: 4 (over z_lo), col: 4 (over y).
Axes of the slice: x: 4, y: 4, z: 8 (z_hi: 2, z_lo: 4; z = z_hi * 4 + z_lo), core: 2. Of those that a mesh axis runs over, the one named last changes fastest.
Arguments:
- atom_feats: bfloat16 [65536, 128], P(('atom', 'row', 'col')), may hold values from -6 to 6
- atom_to_token: int32 [65536], P(('atom', 'row', 'col')), may hold values from 0 to 8191, as said below
- window_start: int32 [2048], P(('atom', 'row', 'col')), may hold values from -64 to 65472, as said below
- atom_bias: bfloat16 [65536, 512], P(('atom', 'row', 'col')), may hold values from -240 to 240
- token_single: bfloat16 [8192, 768], P(('atom', 'row', 'col')), may hold values from -6 to 6
- token_mask: int32 [8192], replicated, may hold values from 0 to 1, as said below
- pair_bias: bfloat16 [16, 8192, 8192], P('atom', 'row', 'col'), may hold values from -240 to 240
- w_atom: bfloat16 [128, 512], replicated, may hold values from -0.5 to 0.5
- w_atom_out: bfloat16 [128, 128], replicated, may hold values from -0.5 to 0.5
- w_to_token: bfloat16 [128, 768], replicated, may hold values from -0.5 to 0.5
- w_token: bfloat16 [768, 3072], replicated, may hold values from -0.21875 to 0.21875
- w_out: bfloat16 [768, 768], P(None, 'col'), may hold values from -0.21875 to 0.21875
Outputs:
- atom_update: bfloat16 [65536, 128], P(('atom', 'row', 'col'))
- token_update: bfloat16 [8192, 768], P(('row', 'atom'), 'col')
Inputs may be any that keep to these rules, and one draw needn't show every extreme that they name: `atom_to_token`: never falls along the atoms; every token owns 1 to 24 atoms and some token of every device's block owns exactly 24; the tokens t with t // 32 = i own exactly the atoms n with n // 256 = i. `window_start`: block b's window starts between 32 * b - 64 and 32 * b - 32. `token_mask`: ones on a leading run of tokens, zeros after it; at least 4096 ones.
All inputs are finite; a program needn't handle non-finite values.
Results may differ from a plain program's by a relative error of at most 0.029.
Values may be sent and summed in bfloat16 or wider, within the bound.
A program may use at most 128 MiB of HBM per device.

v0:
```python
import functools

import jax
import jax.numpy as jnp
from jax import lax
from jax.experimental import pallas as pl
from jax.experimental.pallas import tpu as pltpu
from jax.sharding import PartitionSpec as P

AH = 4
QB = 32
KW = 128
HALO = 64
HD = 48
EPS = 1e-05
NEG = -1e30
BF = jnp.bfloat16
F32 = jnp.float32
MESH = pl.DeviceIdType.MESH
VMEM = pl.BlockSpec(memory_space=pltpu.VMEM)
SMEM = pl.BlockSpec(memory_space=pltpu.SMEM)
NT = (((1,), (1,)), ((), ()))


def layer_norm(values):
    centre = values - jnp.mean(values, axis=-1, keepdims=True)
    spread = jnp.mean(centre * centre, axis=-1, keepdims=True)
    return (centre * lax.rsqrt(spread + EPS)).astype(BF)


def dot(a, b):
    return jnp.dot(a, b, preferred_element_type=F32)


def iota(shape, dim):
    return lax.broadcasted_iota(jnp.int32, shape, dim)


def place():
    return lax.axis_index("atom"), lax.axis_index("row"), lax.axis_index("col")


def atoms(all_atoms, start_ref, feats_ref, before_ref, after_ref, bias_ref, w_atom_ref, device):
    rows, width = feats_ref.shape
    feats = feats_ref[...].astype(F32)
    wide = jnp.concatenate([before_ref[...].astype(F32), feats, after_ref[...].astype(F32)], axis=0)
    proj = dot(layer_norm(wide), w_atom_ref[...])
    queries = proj[HALO : HALO + rows, :width].astype(BF)
    pairs = proj[:, width : 3 * width].astype(BF)
    gate = jax.nn.sigmoid(proj[HALO : HALO + rows, 3 * width :])
    part = width // AH
    reach = KW + QB
    lane_head = iota((QB, width), 1) // part
    ahead = iota((KW, reach), 1) - iota((KW, reach), 0)
    slot = iota((1, KW), 1)
    blocks = []
    for b in range(rows // QB):
        start = start_ref[b]
        shift = start - (device * rows + QB * b) + HALO
        pick = jnp.where(ahead == shift, 1.0, 0.0).astype(BF)
        keyed = dot(pick, pairs[QB * b : QB * b + reach]).astype(BF)
        query = queries[QB * b : QB * (b + 1)]
        stacked = jnp.concatenate(
            [jnp.where(lane_head == h, query, jnp.zeros_like(query)) for h in range(AH)], axis=0
        )
        scores = lax.dot_general(stacked, keyed[:, :width], NT, preferred_element_type=F32)
        bias = jnp.concatenate(
            [bias_ref[QB * b : QB * (b + 1), KW * h : KW * (h + 1)] for h in range(AH)], axis=0
        )
        scores = scores * part ** (-0.5) + bias.astype(F32)
        placed = start + slot
        scores = jnp.where((placed >= 0) & (placed < all_atoms), scores, NEG)
        expo = jnp.exp(scores - jnp.max(scores, axis=-1, keepdims=True))
        weights = (expo / jnp.sum(expo, axis=-1, keepdims=True)).astype(BF)
        mixed = dot(weights, keyed[:, width:])
        block = jnp.zeros((QB, width), F32)
        for h in range(AH):
            block = jnp.where(lane_head == h, mixed[QB * h : QB * (h + 1)], block)
        blocks.append(block)
    return feats, (jnp.concatenate(blocks, axis=0) * gate).astype(BF)


def tokens(member_ref, single_ref, hidden, device):
    toks, rows = single_ref.shape[0], hidden.shape[0]
    local = member_ref[...] - device * toks
    member = jnp.where(local == iota((toks, rows), 0), 1.0, 0.0)
    sums = dot(member.astype(BF), hidden)
    counts = jnp.sum(member, axis=1, keepdims=True)
    return layer_norm(single_ref[...].astype(F32) + sums / counts)


def tiles(head_data, mask_ref, qg_ref, kv_ref, device):
    heads, toks = qg_ref.shape[:2]
    span = 8 * HD
    stacked = jnp.concatenate(
        [head_data[:, span * p : span * (p + 1)] for p in range(heads // 2)], axis=0
    )
    source, target = iota((span, 512), 0), iota((span, 512), 1)
    lane = target % 128
    kind = (target // 128) % 2
    base = (target // 256) * 4 * HD + kind * HD
    first = base + lane
    second = base + jnp.where(kind == 0, 2 * HD, 0) + lane
    wanted = jnp.where(lane < HD, first, jnp.where(lane < 2 * HD, second, -1))
    spread = dot(stacked, jnp.where(source == wanted, 1.0, 0.0).astype(BF))
    live = jnp.sum(jnp.sum(mask_ref[...], axis=0, keepdims=True), axis=1, keepdims=True)
    token = device * toks + iota((toks, 128), 0)
    lanes = iota((toks, 128), 1)
    masked = jnp.where(token < live, 0.0, NEG)
    for h in range(heads):
        rows_h = slice(toks * (h // 2), toks * (h // 2 + 1))
        at = 256 * (h % 2)
        qg = jnp.where(lanes == 2 * HD, 1.0, spread[rows_h, at : at + 128])
        kv = jnp.where(lanes == 2 * HD, masked, spread[rows_h, at + 128 : at + 256])
        kv = jnp.where(lanes == 2 * HD + 1, 1.0, kv)
        qg_ref[h] = qg.astype(BF)
        kv_ref[h] = kv.astype(BF)


def attend(qg, keys_at, bias_at, score_ref, weight_ref, keys_all):
    rows, keys = score_ref.shape
    chunk = 256
    lane = iota((rows, 128), 1)
    query = jnp.where((lane < HD) | (lane == 2 * HD), qg, jnp.zeros_like(qg))
    peak = jnp.full((rows, 128), -jnp.inf, F32)
    for at in range(0, keys, chunk):
        part = lax.dot_general(query, keys_at(at, chunk), NT, preferred_element_type=F32)
        part = part * HD ** (-0.5) + bias_at(at, chunk).astype(F32)
        score_ref[:, at : at + chunk] = part
        for k in range(0, chunk, 128):
            peak = jnp.maximum(peak, part[:, k : k + 128])
    top = jnp.max(peak, axis=1, keepdims=True)
    for at in range(0, keys, chunk):
        weight_ref[:, at : at + chunk] = jnp.exp(score_ref[:, at : at + chunk] - top).astype(BF)
    mixed = dot(weight_ref[...], keys_all())
    total = mixed[:, 2 * HD + 1 : 2 * HD + 2]
    high = top.astype(BF).astype(F32)
    middle = (top - high).astype(BF).astype(F32)
    low = top - high - middle
    total_high = total.astype(BF).astype(F32)
    result = mixed
    for at, value in enumerate((high, middle, low, total_high, total - total_high)):
        result = jnp.where(lane == at, value, result)
    return result.astype(BF)


def merged(parts, gates):
    parts = [p.astype(F32) for p in parts]
    tops = [p[:, 0:1] + p[:, 1:2] + p[:, 2:3] for p in parts]
    totals = [p[:, 3:4] + p[:, 4:5] for p in parts]
    top = functools.reduce(jnp.maximum, tops)
    scales = [jnp.exp(t - top) for t in tops]
    total = sum(s * t for s, t in zip(scales, totals))
    mixed = sum(s * p for s, p in zip(scales, parts))
    attended = jnp.transpose(mixed / total * jax.nn.sigmoid(gates.astype(F32)))
    return attended[HD : 2 * HD].astype(BF)


def unless(own, remote, local):
    @pl.when(jnp.logical_not(own))
    def _():
        remote()

    @pl.when(own)
    def _():
        local()


def whole_kernel(
    all_atoms,
    start_ref,
    feats_in,
    before_in,
    after_in,
    w_atom_in,
    bias_in,
    w_atom_out_in,
    w_to_token_in,
    member_in,
    single_in,
    w_token_in,
    mask_in,
    pair_in,
    w_out_in,
    update_ref,
    out_ref,
    feats_ref,
    before_ref,
    after_ref,
    w_atom_ref,
    bias_ref,
    w_atom_out_ref,
    w_to_token_ref,
    member_ref,
    single_ref,
    w_token_ref,
    mask_ref,
    pair_ref,
    w_out_ref,
    qg_ref,
    kv_ref,
    qall_ref,
    kall_ref,
    score_ref,
    weight_ref,
    part_ref,
    got_ref,
    head_ref,
    all_ref,
    load,
    send,
    q_sem,
    k_sem,
    g_send,
    gq_sem,
    gk_sem,
    m_send,
    m_recv,
    h_send,
    h_recv,
):
    a, r, c = place()
    n_atom, n_row, n_col = (lax.axis_size(x) for x in ("atom", "row", "col"))
    group_q, group_k = n_atom // n_row, n_atom // n_col
    device = (a * n_row + r) * n_col + c
    barrier = pltpu.get_barrier_semaphore()
    loads = [
        pltpu.make_async_copy(source, target, load.at[i])
        for i, (source, target) in enumerate(
            (
                (feats_in, feats_ref),
                (before_in, before_ref),
                (after_in, after_ref),
                (w_atom_in, w_atom_ref),
                (bias_in, bias_ref),
                (w_atom_out_in, w_atom_out_ref),
                (w_to_token_in, w_to_token_ref),
                (member_in, member_ref),
                (single_in, single_ref),
                (w_token_in, w_token_ref),
                (mask_in, mask_ref),
                (pair_in, pair_ref),
                (w_out_in, w_out_ref),
            )
        )
    ]
    for copy in loads:
        copy.start()

    def signal(to):
        pl.semaphore_signal(barrier, inc=1, device_id=to, device_id_type=MESH)

    own_q = a // group_q == r
    own_k = a // group_k == c

    def greet(i, carry):
        source_k = (group_k * c + i // n_col, r, i % n_col)

        @pl.when(jnp.logical_not(own_k & (source_k[0] == a) & (source_k[2] == c)))
        def _():
            signal(source_k)

        source_q = (group_q * r + i // n_row, i % n_row, c)

        @pl.when(jnp.logical_not(own_q & (source_q[0] == a) & (source_q[1] == r)))
        def _():
            signal(source_q)

        @pl.when(jnp.logical_not(own_k & (i == a)))
        def _():
            signal((i, r, a // group_k))

        return carry

    lax.fori_loop(0, n_atom, greet, 0)
    for step in range(1, n_col):
        signal((a, r, lax.rem(c + step, n_col)))
    for step in range(1, n_row):
        signal((a, lax.rem(r + step, n_row), c))

    for copy in loads[:5]:
        copy.wait()
    feats, gated = atoms(
        all_atoms, start_ref, feats_ref, before_ref, after_ref, bias_ref, w_atom_ref, device
    )
    for copy in loads[5:9]:
        copy.wait()
    change = dot(gated, w_atom_out_ref[...])
    update_ref[...] = change.astype(BF)
    hidden = jnp.maximum(dot((feats + change).astype(BF), w_to_token_ref[...]), 0.0).astype(BF)
    normed = tokens(member_ref, single_ref, hidden, device)
    for copy in loads[9:11]:
        copy.wait()
    head_data = dot(normed, w_token_ref[...]).astype(BF)
    tiles(head_data, mask_ref, qg_ref, kv_ref, device)

    count = 3 * n_atom + (n_col - 1) + (n_row - 1)
    pl.semaphore_wait(barrier, count - own_q.astype(jnp.int32) - 2 * own_k.astype(jnp.int32))

    q_slot = lax.rem(a, group_q) * n_row + r
    k_four = lax.rem(a, group_k)
    k_slot = k_four * n_col + c

    def q_copy(to):
        return pltpu.make_async_remote_copy(
            src_ref=qg_ref.at[to],
            dst_ref=qall_ref.at[q_slot, c],
            send_sem=send.at[0, to],
            recv_sem=q_sem.at[q_slot],
            device_id=(to, a // group_q, c),
            device_id_type=MESH,
        )

    def k_copy(to):
        return pltpu.make_async_remote_copy(
            src_ref=kv_ref.at[to],
            dst_ref=kall_ref.at[k_four, r, c],
            send_sem=send.at[1, to],
            recv_sem=k_sem.at[k_slot],
            device_id=(to, r, a // group_k),
            device_id_type=MESH,
        )

    def start(i, carry):
        half = n_atom // 2
        to = lax.rem(a // half + 1 + i // half, 2) * half + lax.rem(a + i, half)
        unless(
            own_k & (to == a),
            lambda: k_copy(to).start(),
            lambda: pltpu.make_async_copy(
                kv_ref.at[to], kall_ref.at[k_four, r, c], k_sem.at[k_slot]
            ).start(),
        )
        unless(
            own_q & (to == a),
            lambda: q_copy(to).start(),
            lambda: pltpu.make_async_copy(
                qg_ref.at[to], qall_ref.at[q_slot, c], q_sem.at[q_slot]
            ).start(),
        )
        return carry

    lax.fori_loop(0, n_atom, start, 0)

    def arrive_k(i, carry):
        pltpu.make_async_copy(
            kv_ref.at[0], kall_ref.at[i // n_col, r, i % n_col], k_sem.at[i]
        ).wait()
        return carry

    def arrive_q(i, carry):
        pltpu.make_async_copy(qg_ref.at[0], qall_ref.at[i, c], q_sem.at[i]).wait()
        return carry

    def gather_q(step):
        mine = qall_ref.at[:, c]
        return pltpu.make_async_remote_copy(
            src_ref=mine,
            dst_ref=mine,
            send_sem=g_send.at[0, step],
            recv_sem=gq_sem.at[step],
            device_id=(a, r, lax.rem(c + step, n_col)),
            device_id_type=MESH,
        )

    def gather_k(step):
        mine = kall_ref.at[:, r]
        return pltpu.make_async_remote_copy(
            src_ref=mine,
            dst_ref=mine,
            send_sem=g_send.at[1, step],
            recv_sem=gk_sem.at[step],
            device_id=(a, lax.rem(r + step, n_row), c),
            device_id_type=MESH,
        )

    lax.fori_loop(0, n_atom, arrive_k, 0)
    for step in range(1, n_row):
        gather_k(step).start()
    lax.fori_loop(0, n_atom, arrive_q, 0)
    for step in range(1, n_col):
        gather_q(step).start()
    for step in range(1, n_col):
        gather_q(step).wait_recv()
    for step in range(1, n_row):
        gather_k(step).wait_recv()
    for copy in loads[11:]:
        copy.wait()

    tile_rows, keys = score_ref.shape
    q_rows = pair_ref.shape[1]
    per_slot = q_rows // n_atom
    per_tile = tile_rows // per_slot
    per_chunk = q_rows // n_col // tile_rows

    def keys_at(at, chunk):
        slots = chunk // per_slot
        index = at // per_slot
        block = kall_ref[index // n_row, index % n_row : index % n_row + slots]
        return block.reshape(chunk, 128)

    def partial(step):
        to = lax.rem(c + step, n_col)
        return pltpu.make_async_remote_copy(
            src_ref=part_ref.at[to],
            dst_ref=got_ref.at[step],
            send_sem=m_send.at[step],
            recv_sem=m_recv.at[step],
            device_id=(a, r, to),
            device_id_type=MESH,
        )

    def one_tile(i, carry):
        step = i // per_chunk + 1
        to = lax.rem(c + step, n_col)
        inner = lax.rem(i, per_chunk)
        index = to * per_chunk + inner
        span = pl.ds(pl.multiple_of(index * tile_rows, tile_rows), tile_rows)
        part_ref[to, pl.ds(pl.multiple_of(inner * tile_rows, tile_rows), tile_rows)] = attend(
            qall_ref[pl.ds(index * per_tile, per_tile)].reshape(tile_rows, 128),
            keys_at,
            lambda at, chunk: pair_ref[0, span, at : at + chunk],
            score_ref,
            weight_ref,
            lambda: kall_ref[...].reshape(keys, 128),
        )

        @pl.when((inner == per_chunk - 1) & (step < n_col))
        def _():
            partial(step).start()

        return carry

    lax.fori_loop(0, n_col * per_chunk, one_tile, 0)
    for step in range(1, n_col):
        partial(step).wait_recv()

    def head_copy(j, k):
        return pltpu.make_async_remote_copy(
            src_ref=head_ref.at[j],
            dst_ref=all_ref.at[a],
            send_sem=h_send.at[j, k],
            recv_sem=h_recv.at[a],
            device_id=(group_k * c + j, r, lax.rem(c + k, n_col)),
            device_id_type=MESH,
        )

    rows = head_ref.shape[2]

    def one_head(j, carry):
        span = pl.ds(pl.multiple_of(j * rows, rows), rows)
        gates = qall_ref[c * group_k + j].reshape(rows, 128)
        parts = [part_ref[c, span]] + [got_ref[step, span] for step in range(1, n_col)]
        head_ref[j] = merged(parts, gates)
        for k in range(1, n_col):
            head_copy(j, k).start()
        unless(
            own_k & (group_k * c + j == a),
            lambda: head_copy(j, 0).start(),
            lambda: pltpu.make_async_copy(head_ref.at[j], all_ref.at[a], h_recv.at[a]).start(),
        )
        return carry

    lax.fori_loop(0, group_k, one_head, 0)

    def arrive(i, carry):
        pltpu.make_async_copy(head_ref.at[0], all_ref.at[i], h_recv.at[i]).wait()
        return carry

    lax.fori_loop(0, n_atom, arrive, 0)
    heads = all_ref[...].reshape(n_atom * HD, rows)
    out_ref[...] = jnp.transpose(dot(w_out_ref[...], heads)).astype(BF)

    def sent(to, carry):
        @pl.when(jnp.logical_not(own_q & (to == a)))
        def _():
            q_copy(to).wait_send()

        @pl.when(jnp.logical_not(own_k & (to == a)))
        def _():
            k_copy(to).wait_send()

        return carry

    lax.fori_loop(0, n_atom, sent, 0)
    for step in range(1, n_col):
        gather_q(step).wait_send()
        partial(step).wait_send()
    for step in range(1, n_row):
        gather_k(step).wait_send()

    def head_sent(j, carry):
        for k in range(1, n_col):
            head_copy(j, k).wait_send()

        @pl.when(jnp.logical_not(own_k & (group_k * c + j == a)))
        def _():
            head_copy(j, 0).wait_send()

        return carry

    lax.fori_loop(0, group_k, head_sent, 0)


def shards(
    atom_feats,
    atom_to_token,
    window_start,
    atom_bias,
    token_single,
    token_mask,
    pair_bias,
    w_atom,
    w_atom_out,
    w_to_token,
    w_token,
    w_out,
):
    rows, width = atom_feats.shape
    toks = token_single.shape[0]
    axes = ("atom", "row", "col")
    n_atom, n_row, n_col = (lax.axis_size(x) for x in axes)
    devices = n_atom * n_row * n_col
    up = [(i, (i + 1) % devices) for i in range(devices)]
    down = [(j, i) for i, j in up]
    before = lax.ppermute(atom_feats[rows - HALO :], axes, up)
    after = lax.ppermute(atom_feats[:HALO], axes, down)
    q_rows, k_cols = pair_bias.shape[1:]
    out_rows = q_rows // n_atom
    group = n_atom // n_col
    tile_rows = 256
    operands = (
        atom_feats,
        before,
        after,
        w_atom,
        atom_bias,
        w_atom_out,
        w_to_token,
        atom_to_token.reshape(1, rows),
        token_single,
        w_token,
        token_mask.reshape(-1, 128),
        pair_bias,
        w_out.T,
    )
    dma = pltpu.SemaphoreType.DMA
    return pl.pallas_call(
        functools.partial(whole_kernel, rows * devices),
        out_shape=(
            jax.ShapeDtypeStruct((rows, width), BF),
            jax.ShapeDtypeStruct((out_rows, w_out.shape[1]), BF),
        ),
        in_specs=[SMEM] + [pl.BlockSpec(memory_space=pl.ANY)] * len(operands),
        out_specs=(VMEM, VMEM),
        scratch_shapes=[pltpu.VMEM(x.shape, x.dtype) for x in operands]
        + [
            pltpu.VMEM((n_atom, toks, 128), BF),
            pltpu.VMEM((n_atom, toks, 128), BF),
            pltpu.VMEM((n_atom, n_col, toks, 128), BF),
            pltpu.VMEM((group, n_row, n_col, toks, 128), BF),
            pltpu.VMEM((tile_rows, k_cols), F32),
            pltpu.VMEM((tile_rows, k_cols), BF),
            pltpu.VMEM((n_col, q_rows // n_col, 128), BF),
            pltpu.VMEM((n_col, q_rows // n_col, 128), BF),
            pltpu.VMEM((group, HD, out_rows), BF),
            pltpu.VMEM((n_atom, HD, out_rows), BF),
            dma((len(operands),)),
            dma((2, n_atom)),
            dma((n_atom,)),
            dma((n_atom,)),
            dma((2, max(n_row, n_col))),
            dma((n_col,)),
            dma((n_row,)),
            dma((n_col,)),
            dma((n_col,)),
            dma((group, n_col)),
            dma((n_atom,)),
        ],
        compiler_params=pltpu.CompilerParams(
            collective_id=0, has_side_effects=True, vmem_limit_bytes=56 << 20
        ),
    )(window_start, *operands)


def solution(mesh):
    placed = (
        P(("atom", "row", "col"), None),
        P(("atom", "row", "col")),
        P(("atom", "row", "col")),
        P(("atom", "row", "col"), None),
        P(("atom", "row", "col"), None),
        P(),
        P("atom", "row", "col"),
        P(),
        P(),
        P(),
        P(),
        P(None, "col"),
    )
    return jax.shard_map(
        shards,
        mesh=mesh,
        in_specs=placed,
        out_specs=(P(("atom", "row", "col"), None), P(("row", "atom"), "col")),
        check_vma=False,
    )
```

profile of v0, /device:TPU:1, one launch (start us, length us, event | category | flops | bytes accessed | tf_op | source)
XLA Modules:
  0.0 72.9 jit_solution(16408248437958815913)
XLA Ops:
  0.6 0.7 %fusion = (bf16[64,128]{1,0:T(8,128)(2,1)S(1)}, bf16[64,128]{1,0:T(8,128)(2,1)S(1)}) fusion(bf16[256,128]{1,0:T(8,128)(2,1)} %feats_in.1), kind=kLoop, calls=%fused_computation | loop fusion | bytes 65536 | tf_op jit(solution)/shard_map/slice | solution.py:527
  1.4 8.2 %collective-permute-start.1 = (bf16[64,128]{1,0:T(8,128)(2,1)S(1)}, bf16[64,128]{1,0:T(8,128)(2,1)S(1)}, u32[]{:S(2)}, u32[]{:S(2)}) collective-permute-start(bf16[64,128]{1,0:T(8,128)(2,1)S(1)} %get-tuple-element.4), channel_id=1, source_target_pairs={{1,0},{2,1},{3,2},{4,3},{5,4},{6,5},{7,6},{8,7},{9,8},{10,9},{11,1... | collective-permute-start | bytes 49160 | tf_op jit(solution)/shard_map/ppermute | solution.py:527
  9.6 0.0 collective-permute-start
  9.6 0.9 %collective-permute-done.1.after_in = bf16[64,128]{1,0:T(8,128)(2,1)S(1)} collective-permute-done((bf16[64,128]{1,0:T(8,128)(2,1)S(1)}, bf16[64,128]{1,0:T(8,128)(2,1)S(1)}, u32[]{:S(2)}, u32[]{:S(2)}) %collective-permute-start.1) | collective-permute-done | bytes 16416 | tf_op jit(solution)/shard_map/ppermute | solution.py:527
  10.4 0.0 copy-start
  10.4 6.3 %collective-permute-done.before_in = bf16[64,128]{1,0:T(8,128)(2,1)S(1)} collective-permute-done((bf16[64,128]{1,0:T(8,128)(2,1)S(1)}, bf16[64,128]{1,0:T(8,128)(2,1)S(1)}, u32[]{:S(2)}, u32[]{:S(2)}) %collective-permute-start) | collective-permute-done | bytes 16416 | tf_op jit(solution)/shard_map/ppermute | solution.py:526
  16.8 0.0 copy-start.1
  16.8 0.0 copy-done
  16.8 0.6 copy-done.1
  17.4 52.5 %shard_map.131 = (bf16[256,128]{1,0:T(8,128)(2,1)}, bf16[128,192]{1,0:T(8,128)(2,1)}) custom-call(s32[8]{0:T(128)} %start_ref.1, bf16[256,128]{1,0:T(8,128)(2,1)} %feats_in.1, bf16[64,128]{1,0:T(8,128)(2,1)} %copy-done.1, bf16[64,128]{1,0:T(8,128)(2,1)} %copy-done, bf16[128,512]{1,0:T(8,128)(2,1)} %w_atom_in.1, bf16[256,512]{1,0:T(8,128)(2,1)} %bias_in.1, ...), custom_call_target="tpu_custom_call" | custom-call | tf_op jit(solution)/shard_map/pallas_call | solution.py:548
  69.9 1.6 %copy.14 = bf16[128,192]{0,1:T(8,128)(2,1)} copy(bf16[128,192]{1,0:T(8,128)(2,1)} %get-tuple-element.3) | data formatting | bytes 98304 | tf_op jit(solution)/shard_map/pallas_call | solution.py:548
  71.4 1.5 %copy.16 = bf16[256,128]{1,0:T(8,128)(2,1)} copy(bf16[256,128]{1,0:T(8,128)(2,1)} %get-tuple-element.8) | data formatting | bytes 131072
Async XLA Ops:
  1.4 9.1 %collective-permute-start.1 = (bf16[64,128]{1,0:T(8,128)(2,1)S(1)}, bf16[64,128]{1,0:T(8,128)(2,1)S(1)}, u32[]{:S(2)}, u32[]{:S(2)}) collective-permute-start(bf16[64,128]{1,0:T(8,128)(2,1)S(1)} %get-tuple-element.4), channel_id=1, source_target_pairs={{1,0},{2,1},{3,2},{4,3},{5,4},{6,5},{7,6},{8,7},{9,8},{10,9},{11,1... | collective-permute-start | bytes 49160 | tf_op jit(solution)/shard_map/ppermute | solution.py:527
  9.6 7.2 %collective-permute-start = (bf16[64,128]{1,0:T(8,128)(2,1)S(1)}, bf16[64,128]{1,0:T(8,128)(2,1)S(1)}, u32[]{:S(2)}, u32[]{:S(2)}) collective-permute-start(bf16[64,128]{1,0:T(8,128)(2,1)S(1)} %get-tuple-element.5), channel_id=1, source_target_pairs={{0,1},{1,2},{2,3},{3,4},{4,5},{5,6},{6,7},{7,8},{8,9},{9,10},{10,1... | collective-permute-start | bytes 49160 | tf_op jit(solution)/shard_map/ppermute | solution.py:526
  10.4 6.3 %copy-start = (bf16[64,128]{1,0:T(8,128)(2,1)}, bf16[64,128]{1,0:T(8,128)(2,1)S(1)}, u32[]{:S(2)}) copy-start(bf16[64,128]{1,0:T(8,128)(2,1)S(1)} %collective-permute-done.1.after_in) | copy-start | bytes 49156
  16.8 0.6 copy-start.1
where the time goes:
time: 74.4 us; the launch traced here: 72.9 us
  Pallas kernels  52.5 us (71%)
  starting transfers between devices  8.19 us (11%)
  waiting for transfers between devices  7.2 us (10%)
  local copies, waits for them, and re-layouts  4.38 us (6%)
    pallas_call x1, Pallas kernels, shards(): pl.pallas_call(functools.partial(whole_kernel, rows * devices), out_shape...  52.5 us
    ppermute x1, starting transfers between devices, shards(): after = lax.ppermute(atom_feats[:HALO], axes, down)  8.19 us
    ppermute x1, waiting for transfers between devices, shards(): before = lax.ppermute(atom_feats[rows - HALO:], axes, up)  6.33 us
    unnamed x5, local copies, waits for them, and re-layouts  2.08 us
    pallas_call x1, local copies, waits for them, and re-layouts, shards(): pl.pallas_call(functools.partial(whole_kernel, rows * devices), out_shape...  1.56 us
  transfers between devices with their start and end apart: 2, of which 2 were waited for; matrix products, arithmetic and copies ran while one was open for 0% of the time, Pallas kernels for 0%

commit v1 on v0

v1 whole, which is shorter than its diff:
```python
import functools

import jax
import jax.numpy as jnp
from jax import lax
from jax.experimental import pallas as pl
from jax.experimental.pallas import tpu as pltpu
from jax.sharding import PartitionSpec as P

AH = 4
QB = 32
KW = 128
HALO = 64
HD = 48
EPS = 1e-05
NEG = -1e30
BF = jnp.bfloat16
F32 = jnp.float32
MESH = pl.DeviceIdType.MESH
VMEM = pl.BlockSpec(memory_space=pltpu.VMEM)
SMEM = pl.BlockSpec(memory_space=pltpu.SMEM)
NT = (((1,), (1,)), ((), ()))


def layer_norm(values):
    centre = values - jnp.mean(values, axis=-1, keepdims=True)
    spread = jnp.mean(centre * centre, axis=-1, keepdims=True)
    return (centre * lax.rsqrt(spread + EPS)).astype(BF)


def dot(a, b):
    return jnp.dot(a, b, preferred_element_type=F32)


def iota(shape, dim):
    return lax.broadcasted_iota(jnp.int32, shape, dim)


def place():
    return lax.axis_index("atom"), lax.axis_index("row"), lax.axis_index("col")


def project(feats, w_atom_ref, first, last):
    return dot(layer_norm(feats.astype(F32)), w_atom_ref[:, first:last])


def window(b, all_atoms, first_atom, start, query, pairs, bias_ref):
    width = query.shape[1]
    part = width // AH
    lane_head = iota((QB, width), 1) // part
    shift = start - (first_atom + QB * b) + HALO
    reach = pairs.shape[0]
    ahead = iota((KW, reach), 1) - iota((KW, reach), 0)
    pick = jnp.where(ahead == shift, 1.0, 0.0).astype(BF)
    keyed = dot(pick, pairs).astype(BF)
    stacked = jnp.concatenate(
        [jnp.where(lane_head == h, query, jnp.zeros_like(query)) for h in range(AH)], axis=0
    )
    scores = lax.dot_general(stacked, keyed[:, :width], NT, preferred_element_type=F32)
    bias = jnp.concatenate(
        [bias_ref[QB * b : QB * (b + 1), KW * h : KW * (h + 1)] for h in range(AH)], axis=0
    )
    scores = scores * part ** (-0.5) + bias.astype(F32)
    placed = start + iota((1, KW), 1)
    scores = jnp.where((placed >= 0) & (placed < all_atoms), scores, NEG)
    expo = jnp.exp(scores - jnp.max(scores, axis=-1, keepdims=True))
    weights = (expo / jnp.sum(expo, axis=-1, keepdims=True)).astype(BF)
    mixed = dot(weights, keyed[:, width:])
    block = mixed[:QB]
    for h in range(1, AH):
        block = jnp.where(lane_head == h, mixed[QB * h : QB * (h + 1)], block)
    return block


def tokens(member_ref, single_ref, hidden, device):
    toks, rows = single_ref.shape[0], hidden.shape[0]
    local = member_ref[...] - device * toks
    member = jnp.where(local == iota((toks, rows), 0), 1.0, 0.0)
    sums = dot(member.astype(BF), hidden)
    counts = jnp.sum(member, axis=1, keepdims=True)
    return layer_norm(single_ref[...].astype(F32) + sums / counts)


def tiles(head_data, mask_ref, qg_ref, kv_ref, device):
    heads, toks = qg_ref.shape[:2]
    span = 8 * HD
    stacked = jnp.concatenate(
        [head_data[:, span * p : span * (p + 1)] for p in range(heads // 2)], axis=0
    )
    source, target = iota((span, 512), 0), iota((span, 512), 1)
    lane = target % 128
    kind = (target // 128) % 2
    base = (target // 256) * 4 * HD
    first = base + jnp.where(kind == 0, 3 * HD, 2 * HD) + lane
    second = base + jnp.where(kind == 0, 0, HD) + lane - HD
    wanted = jnp.where(lane < HD, first, jnp.where(lane < 2 * HD, second, -1))
    spread = dot(stacked, jnp.where(source == wanted, 1.0, 0.0).astype(BF))
    live = jnp.sum(jnp.sum(mask_ref[...], axis=0, keepdims=True), axis=1, keepdims=True)
    token = device * toks + iota((toks, 128), 0)
    lanes = iota((toks, 128), 1)
    masked = jnp.where(token < live, 0.0, NEG)
    for h in range(heads):
        rows_h = slice(toks * (h // 2), toks * (h // 2 + 1))
        at = 256 * (h % 2)
        qg = jnp.where(lanes == 2 * HD, 1.0, spread[rows_h, at : at + 128])
        kv = jnp.where(lanes == 2 * HD, masked, spread[rows_h, at + 128 : at + 256])
        kv = jnp.where(lanes == 2 * HD + 1, 1.0, kv)
        qg_ref[h] = qg.astype(BF)
        kv_ref[h] = kv.astype(BF)


def summary(mixed, top):
    lane = iota(mixed.shape, 1)
    total = mixed[:, 2 * HD + 1 : 2 * HD + 2]
    high = top.astype(BF).astype(F32)
    middle = (top - high).astype(BF).astype(F32)
    total_high = total.astype(BF).astype(F32)
    for at, value in enumerate((high, middle, top - high - middle, total_high, total - total_high)):
        mixed = jnp.where(lane == HD + at, value, mixed)
    return mixed


def paired(first, second):
    return jnp.where(iota(first.shape, 1) < 64, first, pltpu.roll(second, 64, 1))


def merged(parts, gates):
    parts = [p.astype(F32) for p in parts]
    scales, totals = [], []
    for at in (HD, 64 + HD):
        tops = [p[:, at : at + 1] + p[:, at + 1 : at + 2] + p[:, at + 2 : at + 3] for p in parts]
        counts = [p[:, at + 3 : at + 4] + p[:, at + 4 : at + 5] for p in parts]
        top = functools.reduce(jnp.maximum, tops)
        scales.append([jnp.exp(t - top) for t in tops])
        totals.append(sum(s * t for s, t in zip(scales[-1], counts)))
    low = iota(parts[0].shape, 1) < 64
    mixed = sum(jnp.where(low, s, t) * p for s, t, p in zip(*scales, parts))
    attended = mixed / jnp.where(low, *totals) * jax.nn.sigmoid(gates)
    return jnp.transpose(attended).astype(BF)


def unless(own, remote, local):
    @pl.when(jnp.logical_not(own))
    def _():
        remote()

    @pl.when(own)
    def _():
        local()


def whole_kernel(
    all_atoms,
    start_ref,
    feats_in,
    w_atom_in,
    bias_in,
    w_atom_out_in,
    w_to_token_in,
    member_in,
    single_in,
    w_token_in,
    mask_in,
    pair_in,
    w_out_in,
    out_ref,
    feats_ref,
    w_atom_ref,
    bias_ref,
    w_atom_out_ref,
    w_to_token_ref,
    member_ref,
    single_ref,
    w_token_ref,
    mask_ref,
    pair_ref,
    w_out_ref,
    halo_ref,
    mixed_ref,
    qg_ref,
    kv_ref,
    qall_ref,
    kall_ref,
    query_ref,
    peak_ref,
    score_ref,
    weight_ref,
    part_ref,
    got_ref,
    head_ref,
    all_ref,
    load,
    halo_send,
    halo_recv,
    send,
    q_sem,
    k_sem,
    g_send,
    gq_sem,
    gk_sem,
    m_send,
    m_recv,
    h_send,
    h_recv,
):
    a, r, c = place()
    n_atom, n_row, n_col = (lax.axis_size(x) for x in ("atom", "row", "col"))
    group_q, group_k = n_atom // n_row, n_atom // n_col
    devices = n_atom * n_row * n_col
    device = (a * n_row + r) * n_col + c
    rows = feats_ref.shape[0]
    barrier = pltpu.get_barrier_semaphore()
    loads = [
        pltpu.make_async_copy(source, target, load.at[i])
        for i, (source, target) in enumerate(
            (
                (feats_in, feats_ref),
                (w_atom_in, w_atom_ref),
                (bias_in, bias_ref),
                (w_atom_out_in, w_atom_out_ref),
                (w_to_token_in, w_to_token_ref),
                (member_in, member_ref),
                (single_in, single_ref),
                (w_token_in, w_token_ref),
                (mask_in, mask_ref),
                (pair_in, pair_ref),
                (w_out_in, w_out_ref),
            )
        )
    ]
    for copy in loads:
        copy.start()

    def signal(to):
        pl.semaphore_signal(barrier, inc=1, device_id=to, device_id_type=MESH)

    own_q = a // group_q == r
    own_k = a // group_k == c
    own_h = lax.rem(a, n_row) == c

    def greet(i, carry):
        source_k = (group_k * c + i // n_col, r, i % n_col)

        @pl.when(jnp.logical_not(own_k & (source_k[0] == a) & (source_k[2] == c)))
        def _():
            signal(source_k)

        source_q = (group_q * r + i // n_row, i % n_row, c)

        @pl.when(jnp.logical_not(own_q & (source_q[0] == a) & (source_q[1] == r)))
        def _():
            signal(source_q)

        @pl.when(jnp.logical_not(own_h & (i == a)))
        def _():
            signal((i, r, lax.rem(a, n_row)))

        return carry

    lax.fori_loop(0, n_atom, greet, 0)
    for step in range(1, n_col):
        signal((a, r, lax.rem(c + step, n_col)))
    for step in range(1, n_row):
        signal((a, lax.rem(r + step, n_row), c))
    for step in (1, devices - 1):
        other = lax.rem(device + step, devices)
        signal((other // (n_row * n_col), lax.rem(other // n_col, n_row), lax.rem(other, n_col)))

    def halo_copy(side):
        other = lax.rem(device + (1 if side == 0 else devices - 1), devices)
        edge = rows - HALO if side == 0 else 0
        return pltpu.make_async_remote_copy(
            src_ref=feats_in.at[pl.ds(edge, HALO)],
            dst_ref=halo_ref.at[side],
            send_sem=halo_send.at[side],
            recv_sem=halo_recv.at[side],
            device_id=(
                other // (n_row * n_col),
                lax.rem(other // n_col, n_row),
                lax.rem(other, n_col),
            ),
            device_id_type=MESH,
        )

    def drain_halo():
        for side in range(2):
            halo_copy(side).wait_send()

    for copy in loads[:3]:
        copy.wait()
    rows, width = feats_ref.shape
    first_atom = device * rows
    with jax.named_scope("inner_windows"):
        feats = feats_ref[...]
        proj = project(feats, w_atom_ref, 0, 4 * width)
        queries = proj[:, :width].astype(BF)
        pairs = proj[:, width : 3 * width].astype(BF)
        gate = jax.nn.sigmoid(proj[:, 3 * width :])
        edge = HALO // QB
        blocks = rows // QB
        inner = range(edge, blocks - edge)

        def one_window(b, reach):
            query = queries[QB * b : QB * (b + 1)]
            mixed_ref[QB * b : QB * (b + 1)] = window(
                b, all_atoms, first_atom, start_ref[b], query, reach, bias_ref
            )

        for b in inner:
            one_window(b, pairs[QB * (b - edge) : QB * (b + edge + 1)])
    with jax.named_scope("barrier"):
        count = 3 * n_atom + (n_col - 1) + (n_row - 1) + 2
        for own in (own_q, own_k, own_h):
            count = count - own.astype(jnp.int32)
        pl.semaphore_wait(barrier, count)
    with jax.named_scope("halo"):
        for side in range(2):
            halo_copy(side).start()
        for side in range(2):
            halo_copy(side).wait_recv()
    with jax.named_scope("outer_windows"):
        around = project(halo_ref[...].reshape(2 * HALO, width), w_atom_ref, width, 3 * width)
        around = around.astype(BF)
        before, after = around[:HALO], around[HALO:]
        wide = jnp.concatenate([before, pairs[: QB * 2 * edge]], axis=0)
        for b in range(edge):
            one_window(b, wide[QB * b : QB * (b + 2 * edge + 1)])
        wide = jnp.concatenate([pairs[rows - QB * 2 * edge :], after], axis=0)
        for b in range(edge):
            one_window(blocks - edge + b, wide[QB * b : QB * (b + 2 * edge + 1)])
        gated = (mixed_ref[...] * gate).astype(BF)
    with jax.named_scope("tokens"):
        for copy in loads[3:7]:
            copy.wait()
        change = dot(gated, w_atom_out_ref[...])
        out_ref[:rows] = change.astype(BF)
        acted = (feats.astype(F32) + change).astype(BF)
        hidden = jnp.maximum(dot(acted, w_to_token_ref[...]), 0.0).astype(BF)
        normed = tokens(member_ref, single_ref, hidden, device)
        for copy in loads[7:9]:
            copy.wait()
        head_data = dot(normed, w_token_ref[...]).astype(BF)
        tiles(head_data, mask_ref, qg_ref, kv_ref, device)

    q_slot = lax.rem(a, group_q) * n_row + r
    k_four = lax.rem(a, group_k)
    k_slot = k_four * n_col + c

    def q_copy(to):
        return pltpu.make_async_remote_copy(
            src_ref=qg_ref.at[to],
            dst_ref=qall_ref.at[q_slot, c],
            send_sem=send.at[0, to],
            recv_sem=q_sem.at[q_slot],
            device_id=(to, a // group_q, c),
            device_id_type=MESH,
        )

    def k_copy(to):
        return pltpu.make_async_remote_copy(
            src_ref=kv_ref.at[to],
            dst_ref=kall_ref.at[r, k_four, c],
            send_sem=send.at[1, to],
            recv_sem=k_sem.at[k_slot],
            device_id=(to, r, a // group_k),
            device_id_type=MESH,
        )

    def drain_tiles():
        def sent(to, carry):
            unless(own_q & (to == a), lambda: q_copy(to).wait_send(), lambda: None)
            unless(own_k & (to == a), lambda: k_copy(to).wait_send(), lambda: None)
            return carry

        lax.fori_loop(0, n_atom, sent, 0)

    def start(i, carry):
        half = n_atom // 2
        to = lax.rem(a // half + 1 + i // half, 2) * half + lax.rem(a + i, half)
        unless(
            own_k & (to == a),
            lambda: k_copy(to).start(),
            lambda: pltpu.make_async_copy(
                kv_ref.at[to], kall_ref.at[r, k_four, c], k_sem.at[k_slot]
            ).start(),
        )
        unless(
            own_q & (to == a),
            lambda: q_copy(to).start(),
            lambda: pltpu.make_async_copy(
                qg_ref.at[to], qall_ref.at[q_slot, c], q_sem.at[q_slot]
            ).start(),
        )
        return carry

    with jax.named_scope("send_tiles"):
        lax.fori_loop(0, n_atom, start, 0)

    def arrive_k(i, carry):
        pltpu.make_async_copy(
            kv_ref.at[0], kall_ref.at[r, i // n_col, i % n_col], k_sem.at[i]
        ).wait()
        return carry

    def arrive_q(i, carry):
        pltpu.make_async_copy(qg_ref.at[0], qall_ref.at[i, c], q_sem.at[i]).wait()
        return carry

    def gather_q(step):
        mine = qall_ref.at[:, c]
        return pltpu.make_async_remote_copy(
            src_ref=mine,
            dst_ref=mine,
            send_sem=g_send.at[0, step],
            recv_sem=gq_sem.at[step],
            device_id=(a, r, lax.rem(c + step, n_col)),
            device_id_type=MESH,
        )

    def partner(step):
        half = n_row // 2
        return lax.rem(r // 2 + step // 2, half) * 2 + lax.rem(lax.rem(r, 2) + step % 2, 2)

    def gather_k(step):
        return pltpu.make_async_remote_copy(
            src_ref=kall_ref.at[r],
            dst_ref=kall_ref.at[r],
            send_sem=g_send.at[1, step],
            recv_sem=gk_sem.at[step],
            device_id=(a, partner(step), c),
            device_id_type=MESH,
        )

    def drain_gather():
        for step in range(1, n_col):
            gather_q(step).wait_send()
        for step in range(1, n_row):
            gather_k(step).wait_send()

    with jax.named_scope("tiles_arrive"):
        lax.fori_loop(0, n_atom, arrive_q, 0)
        for step in range(1, n_col):
            gather_q(step).start()
        lax.fori_loop(0, n_atom, arrive_k, 0)
        for step in range(1, n_row):
            gather_k(step).start()
    for copy in loads[9:]:
        copy.wait()
    with jax.named_scope("gather_q"):
        for step in range(1, n_col):
            gather_q(step).wait_recv()
    q_rows, keys = pair_ref.shape[1:]
    per_slot = q_rows // n_atom
    per_row = keys // n_row
    lane = iota((q_rows, 128), 1)
    queries = qall_ref[...].reshape(q_rows, 128)
    query_ref[...] = jnp.where(
        (lane >= HD) & (lane <= 2 * HD), queries, jnp.zeros_like(queries)
    )
    peak_ref[...] = jnp.full_like(peak_ref, -jnp.inf)

    def score(step, carry):
        source = partner(step)

        @pl.when(step > 0)
        def _():
            mine = kall_ref.at[source]
            pltpu.make_async_copy(mine, mine, gk_sem.at[step]).wait()

        held = kall_ref[source].reshape(per_row, 128)
        half = q_rows // 2
        span = half // (n_row * per_slot)
        for i in range(2):
            rows = slice(half * i, half * (i + 1))
            fours = slice(span * i, span * (i + 1))
            peak = peak_ref[fours]
            for at in range(0, per_row, 256):
                part = lax.dot_general(
                    query_ref[rows], held[at : at + 256], NT, preferred_element_type=F32
                )
                for k in range(0, 256, 128):
                    four = (at + k) // 128
                    column = four * per_row + source * 128
                    bias = pair_ref[0, rows, pl.ds(pl.multiple_of(column, 128), 128)]
                    value = part[:, k : k + 128] * HD ** (-0.5) + bias.astype(F32)
                    value = value.reshape(peak.shape)
                    column = source * per_row + at + k
                    score_ref[fours, :, :, pl.ds(pl.multiple_of(column, 128), 128)] = value
                    peak = jnp.maximum(peak, value)
            peak_ref[fours] = peak
        return carry

    with jax.named_scope("scores"):
        lax.fori_loop(0, n_row, score, 0)

    def partial(step):
        to = lax.rem(c + step, n_col)
        return pltpu.make_async_remote_copy(
            src_ref=part_ref.at[to],
            dst_ref=got_ref.at[step],
            send_sem=m_send.at[step],
            recv_sem=m_recv.at[step],
            device_id=(a, r, to),
            device_id_type=MESH,
        )

    def drain_partials():
        for step in range(1, n_col):
            partial(step).wait_send()

    def quarter(i, carry):
        to = lax.rem(c + i + 1, n_col)
        results = []
        for h in range(2):
            fours = slice(2 * h, 2 * h + 2)
            top = jnp.max(peak_ref[fours, to].reshape(2 * per_slot, 128), axis=1, keepdims=True)
            for at in range(0, keys, 256):
                part = score_ref[fours, to, :, at : at + 256].reshape(2 * per_slot, 256)
                weight_ref[h, :, at : at + 256] = jnp.exp(part - top).astype(BF)
            mixed = dot(weight_ref[h], kall_ref[...].reshape(keys, 128))
            results.append(summary(mixed, top))
        part_ref[to] = paired(*results).astype(BF)

        @pl.when(i < n_col - 1)
        def _():
            partial(i + 1).start()

        return carry

    with jax.named_scope("attention"):
        lax.fori_loop(0, n_col, quarter, 0)
    with jax.named_scope("partials_arrive"):
        for step in range(1, n_col):
            partial(step).wait_recv()

    def head_copy(j, k):
        return pltpu.make_async_remote_copy(
            src_ref=head_ref.at[j],
            dst_ref=all_ref.at[a],
            send_sem=h_send.at[j, k],
            recv_sem=h_recv.at[a],
            device_id=(n_row * j + c, r, lax.rem(c + k, n_col)),
            device_id_type=MESH,
        )

    def drain_heads():
        def sent(j, carry):
            for k in range(1, n_col):
                head_copy(j, k).wait_send()
            unless(
                own_h & (n_row * j + c == a),
                lambda: head_copy(j, 0).wait_send(),
                lambda: None,
            )
            return carry

        lax.fori_loop(0, group_k, sent, 0)

    out_rows = head_ref.shape[2]

    def one_head(j, carry):
        for k in range(1, n_col):
            head_copy(j, k).start()
        unless(
            own_h & (n_row * j + c == a),
            lambda: head_copy(j, 0).start(),
            lambda: pltpu.make_async_copy(head_ref.at[j], all_ref.at[a], h_recv.at[a]).start(),
        )
        return carry

    with jax.named_scope("merge"):
        parts = [part_ref[c]] + [got_ref[step] for step in range(1, n_col)]
        gates = [
            jnp.concatenate(
                [qall_ref[n_row * u + c].reshape(per_slot, 128) for u in (2 * h, 2 * h + 1)], axis=0
            ).astype(F32)
            for h in range(2)
        ]
        attended = merged(parts, paired(*gates))
        for u in range(group_k):
            at = 64 * (u // 2)
            head_ref[u] = attended[at : at + HD, out_rows * (u % 2) : out_rows * (u % 2 + 1)]
    with jax.named_scope("send_heads"):
        lax.fori_loop(0, group_k, one_head, 0)

    def arrive(i, carry):
        pltpu.make_async_copy(head_ref.at[0], all_ref.at[i], h_recv.at[i]).wait()
        return carry

    with jax.named_scope("heads_arrive"):
        lax.fori_loop(0, n_atom, arrive, 0)
    with jax.named_scope("output"):
        heads = all_ref[...].reshape(n_atom * HD, head_ref.shape[2])
        out_ref[rows:] = dot(w_out_ref[...], heads).astype(BF)

    drain_halo()
    drain_tiles()
    drain_gather()
    drain_partials()
    drain_heads()


def shards(
    atom_feats,
    atom_to_token,
    window_start,
    atom_bias,
    token_single,
    token_mask,
    pair_bias,
    w_atom,
    w_atom_out,
    w_to_token,
    w_token,
    w_out,
):
    rows, width = atom_feats.shape
    toks = token_single.shape[0]
    axes = ("atom", "row", "col")
    n_atom, n_row, n_col = (lax.axis_size(x) for x in axes)
    devices = n_atom * n_row * n_col
    q_rows, k_cols = pair_bias.shape[1:]
    out_rows = q_rows // n_atom
    group = n_atom // n_col
    tile_rows = q_rows // n_col // 2
    operands = (
        atom_feats,
        w_atom,
        atom_bias,
        w_atom_out,
        w_to_token,
        atom_to_token.reshape(1, rows),
        token_single,
        w_token,
        token_mask.reshape(-1, 128),
        pair_bias,
        w_out.T,
    )
    dma = pltpu.SemaphoreType.DMA
    both = pl.pallas_call(
        functools.partial(whole_kernel, rows * devices),
        out_shape=jax.ShapeDtypeStruct((rows + w_out.shape[1], out_rows), BF),
        in_specs=[SMEM] + [pl.BlockSpec(memory_space=pl.ANY)] * len(operands),
        out_specs=VMEM,
        scratch_shapes=[pltpu.VMEM(x.shape, x.dtype) for x in operands]
        + [
            pltpu.VMEM((2, HALO, width), BF),
            pltpu.VMEM((rows, width), F32),
            pltpu.VMEM((n_atom, toks, 128), BF),
            pltpu.VMEM((n_atom, toks, 128), BF),
            pltpu.VMEM((n_atom, n_col, toks, 128), BF),
            pltpu.VMEM((n_row, group, n_col, toks, 128), BF),
            pltpu.VMEM((q_rows, 128), BF),
            pltpu.VMEM((group, n_row, out_rows, 128), F32),
            pltpu.VMEM((group, n_row, out_rows, k_cols), F32),
            pltpu.VMEM((2, tile_rows, k_cols), BF),
            pltpu.VMEM((n_col, tile_rows, 128), BF),
            pltpu.VMEM((n_col, tile_rows, 128), BF),
            pltpu.VMEM((group, HD, out_rows), BF),
            pltpu.VMEM((n_atom, HD, out_rows), BF),
            dma((len(operands),)),
            dma((2,)),
            dma((2,)),
            dma((2, n_atom)),
            dma((n_atom,)),
            dma((n_atom,)),
            dma((2, max(n_row, n_col))),
            dma((n_col,)),
            dma((n_row,)),
            dma((n_col,)),
            dma((n_col,)),
            dma((group, n_col)),
            dma((n_atom,)),
        ],
        compiler_params=pltpu.CompilerParams(
            collective_id=0, has_side_effects=True, vmem_limit_bytes=56 << 20
        ),
    )(window_start, *operands)
    return (both[:rows], both[rows:].T)


def solution(mesh):
    placed = (
        P(("atom", "row", "col"), None),
        P(("atom", "row", "col")),
        P(("atom", "row", "col")),
        P(("atom", "row", "col"), None),
        P(("atom", "row", "col"), None),
        P(),
        P("atom", "row", "col"),
        P(),
        P(),
        P(),
        P(),
        P(None, "col"),
    )
    return jax.shard_map(
        shards,
        mesh=mesh,
        in_specs=placed,
        out_specs=(P(("atom", "row", "col"), None), P(("row", "atom"), "col")),
        check_vma=False,
    )
```

time: 74.4 us -> 65.8 us (0.88); the launches traced: 72.9 us -> 65.6 us
  Pallas kernels: 52.5 us -> 62.1 us
  starting transfers between devices: 8.19 us -> 0 us
  waiting for transfers between devices: 7.2 us -> 0 us
  local copies, waits for them, and re-layouts: 4.38 us -> 2.89 us
    pallas_call x1, Pallas kernels: 52.5 us -> 62.1 us  [shards(): pl.pallas_call(functools.partial(whole_kernel, rows * devices), out_shape...]
    ppermute x2 -> x0, starting transfers between devices: 8.19 us -> none  [the longest x1 8.19 us: shards(): after = lax.ppermute(atom_feats[:HALO], axes, down)]
    ppermute x2 -> x0, waiting for transfers between devices: 7.2 us -> none  [the longest x1 6.33 us: shards(): before = lax.ppermute(atom_feats[rows - HALO:], axes, up)]
    unnamed x5 -> x0, local copies, waits for them, and re-layouts: 2.08 us -> none
    pallas_call x1 -> x0, local copies, waits for them, and re-layouts: 1.56 us -> none  [shards(): pl.pallas_call(functools.partial(whole_kernel, rows * devices), out_shape...]
    transpose x0 -> x1, local copies, waits for them, and re-layouts: none -> 1.42 us  [shards(): return (both[:rows], both[rows:].T)]
  transfers between devices with their start and end apart: 2 -> 0, of which waited for: 2 -> 0; matrix products, arithmetic and copies ran while one was open for 0% -> 0% of each run, Pallas kernels for 0% -> 0%
where the time goes in v1:
time: 65.8 us; the launch traced here: 65.6 us
  Pallas kernels  62.1 us (94%)
  local copies, waits for them, and re-layouts  2.89 us (4%)
    pallas_call x1, Pallas kernels, shards(): pl.pallas_call(functools.partial(whole_kernel, rows * devices), out_shape...  62.1 us
    slice x1, local copies, waits for them, and re-layouts, shards(): return (both[:rows], both[rows:].T)  1.47 us
    transpose x1, local copies, waits for them, and re-layouts, shards(): return (both[:rows], both[rows:].T)  1.42 us

profile of v1, /device:TPU:1, one launch (start us, length us, event | category | flops | bytes accessed | tf_op | source)
XLA Modules:
  0.0 65.6 jit_solution(15229794875384423056)
XLA Ops:
  0.6 62.1 %shard_map.131 = bf16[448,128]{1,0:T(8,128)(2,1)} custom-call(s32[8]{0:T(128)} %start_ref.1, bf16[256,128]{1,0:T(8,128)(2,1)} %feats_in.1, bf16[128,512]{1,0:T(8,128)(2,1)} %w_atom_in.1, bf16[256,512]{1,0:T(8,128)(2,1)} %bias_in.1, bf16[128,128]{1,0:T(8,128)(2,1)} %w_atom_out_in.1, bf16[128,768]{1,0:T(8,128)(2,1)} %w_to_token_in.1, s32[1,256]{1,0:T(1,128)} %bitcast.7, ...), custom_call_target="tpu_custom_call" | custom-call | tf_op jit(solution)/shard_map/pallas_call | solution.py:640
  62.7 1.4 %slice_bitcast_fusion = bf16[128,192]{0,1:T(8,128)(2,1)} fusion(bf16[448,128]{1,0:T(8,128)(2,1)} %shard_map.131), kind=kLoop, calls=%fused_computation | loop fusion | bytes 98304 | tf_op jit(solution)/shard_map/transpose | solution.py:679
  64.1 1.5 %slice.6 = bf16[256,128]{1,0:T(8,128)(2,1)} slice(bf16[448,128]{1,0:T(8,128)(2,1)} %shard_map.131), slice={[0:256], [0:128]} | slice | bytes 131072 | tf_op jit(solution)/shard_map/slice | solution.py:679

commit v2 on v1

--- a/solution.py
+++ b/solution.py
@@ -12,6 +12,7 @@
 KW = 128
 HALO = 64
 HD = 48
+LAST = 80
 EPS = 1e-05
 NEG = -1e30
 BF = jnp.bfloat16
@@ -81,59 +82,58 @@
     return layer_norm(single_ref[...].astype(F32) + sums / counts)
 
 
-def tiles(head_data, mask_ref, qg_ref, kv_ref, device):
-    heads, toks = qg_ref.shape[:2]
+def chooser():
     span = 8 * HD
-    stacked = jnp.concatenate(
-        [head_data[:, span * p : span * (p + 1)] for p in range(heads // 2)], axis=0
-    )
     source, target = iota((span, 512), 0), iota((span, 512), 1)
     lane = target % 128
     kind = (target // 128) % 2
     base = (target // 256) * 4 * HD
-    first = base + jnp.where(kind == 0, 3 * HD, 2 * HD) + lane
-    second = base + jnp.where(kind == 0, 0, HD) + lane - HD
-    wanted = jnp.where(lane < HD, first, jnp.where(lane < 2 * HD, second, -1))
-    spread = dot(stacked, jnp.where(source == wanted, 1.0, 0.0).astype(BF))
-    live = jnp.sum(jnp.sum(mask_ref[...], axis=0, keepdims=True), axis=1, keepdims=True)
-    token = device * toks + iota((toks, 128), 0)
-    lanes = iota((toks, 128), 1)
-    masked = jnp.where(token < live, 0.0, NEG)
-    for h in range(heads):
+    first = base + jnp.where(kind == 0, 0, HD) + lane
+    second = base + jnp.where(kind == 0, 3 * HD, 2 * HD) + lane - LAST
+    wanted = jnp.where(lane < HD, first, jnp.where(lane >= LAST, second, -1))
+    return jnp.where(source == wanted, 1.0, 0.0).astype(BF)
+
+
+def tiles(head_data, choose, first, qg_ref, kv_ref):
+    toks, columns = head_data.shape
+    span = 8 * HD
+    pairs = columns // span
+    stacked = jnp.concatenate(
+        [head_data[:, span * p : span * (p + 1)] for p in range(pairs)], axis=0
+    )
+    spread = dot(stacked, choose).astype(BF)
+    for h in range(2 * pairs):
         rows_h = slice(toks * (h // 2), toks * (h // 2 + 1))
         at = 256 * (h % 2)
-        qg = jnp.where(lanes == 2 * HD, 1.0, spread[rows_h, at : at + 128])
-        kv = jnp.where(lanes == 2 * HD, masked, spread[rows_h, at + 128 : at + 256])
-        kv = jnp.where(lanes == 2 * HD + 1, 1.0, kv)
-        qg_ref[h] = qg.astype(BF)
-        kv_ref[h] = kv.astype(BF)
+        qg_ref[first + h] = spread[rows_h, at : at + 128]
+        kv_ref[first + h] = spread[rows_h, at + 128 : at + 256]
 
 
 def summary(mixed, top):
     lane = iota(mixed.shape, 1)
-    total = mixed[:, 2 * HD + 1 : 2 * HD + 2]
+    total = mixed[:, HD + 1 : HD + 2]
     high = top.astype(BF).astype(F32)
     middle = (top - high).astype(BF).astype(F32)
     total_high = total.astype(BF).astype(F32)
     for at, value in enumerate((high, middle, top - high - middle, total_high, total - total_high)):
-        mixed = jnp.where(lane == HD + at, value, mixed)
+        mixed = jnp.where(lane == 64 + at, value, mixed)
     return mixed
 
 
 def paired(first, second):
-    return jnp.where(iota(first.shape, 1) < 64, first, pltpu.roll(second, 64, 1))
+    return jnp.where(iota(first.shape, 1) >= 64, first, pltpu.roll(second, 64, 1))
 
 
 def merged(parts, gates):
     parts = [p.astype(F32) for p in parts]
     scales, totals = [], []
-    for at in (HD, 64 + HD):
+    for at in (64, 0):
         tops = [p[:, at : at + 1] + p[:, at + 1 : at + 2] + p[:, at + 2 : at + 3] for p in parts]
         counts = [p[:, at + 3 : at + 4] + p[:, at + 4 : at + 5] for p in parts]
         top = functools.reduce(jnp.maximum, tops)
         scales.append([jnp.exp(t - top) for t in tops])
         totals.append(sum(s * t for s, t in zip(scales[-1], counts)))
-    low = iota(parts[0].shape, 1) < 64
+    low = iota(parts[0].shape, 1) >= 64
     mixed = sum(jnp.where(low, s, t) * p for s, t, p in zip(*scales, parts))
     attended = mixed / jnp.where(low, *totals) * jax.nn.sigmoid(gates)
     return jnp.transpose(attended).astype(BF)
@@ -179,8 +179,11 @@
     mixed_ref,
     qg_ref,
     kv_ref,
-    qall_ref,
-    kall_ref,
+    qown_ref,
+    kown_ref,
+    qpack_ref,
+    gate_ref,
+    keys_ref,
     query_ref,
     peak_ref,
     score_ref,
@@ -198,6 +201,7 @@
     g_send,
     gq_sem,
     gk_sem,
+    gg_sem,
     m_send,
     m_recv,
     h_send,
@@ -228,7 +232,7 @@
             )
         )
     ]
-    for copy in loads:
+    for copy in loads[:3]:
         copy.start()
 
     def signal(to):
@@ -239,22 +243,9 @@
     own_h = lax.rem(a, n_row) == c
 
     def greet(i, carry):
-        source_k = (group_k * c + i // n_col, r, i % n_col)
-
-        @pl.when(jnp.logical_not(own_k & (source_k[0] == a) & (source_k[2] == c)))
-        def _():
-            signal(source_k)
-
-        source_q = (group_q * r + i // n_row, i % n_row, c)
-
-        @pl.when(jnp.logical_not(own_q & (source_q[0] == a) & (source_q[1] == r)))
-        def _():
-            signal(source_q)
-
-        @pl.when(jnp.logical_not(own_h & (i == a)))
-        def _():
-            signal((i, r, lax.rem(a, n_row)))
-
+        signal((i, r, lax.rem(a, n_row)))
+        signal((group_k * c + i // n_col, r, lax.rem(i, n_col)))
+        signal((group_q * r + i // n_row, lax.rem(i, n_row), c))
         return carry
 
     lax.fori_loop(0, n_atom, greet, 0)
@@ -288,6 +279,8 @@
 
     for copy in loads[:3]:
         copy.wait()
+    for copy in loads[3:9]:
+        copy.start()
     rows, width = feats_ref.shape
     first_atom = device * rows
     with jax.named_scope("inner_windows"):
@@ -308,11 +301,10 @@
 
         for b in inner:
             one_window(b, pairs[QB * (b - edge) : QB * (b + edge + 1)])
+    for copy in loads[9:]:
+        copy.start()
     with jax.named_scope("barrier"):
-        count = 3 * n_atom + (n_col - 1) + (n_row - 1) + 2
-        for own in (own_q, own_k, own_h):
-            count = count - own.astype(jnp.int32)
-        pl.semaphore_wait(barrier, count)
+        pl.semaphore_wait(barrier, 3 * n_atom + (n_col - 1) + (n_row - 1) + 2)
     with jax.named_scope("halo"):
         for side in range(2):
             halo_copy(side).start()
@@ -339,17 +331,17 @@
         normed = tokens(member_ref, single_ref, hidden, device)
         for copy in loads[7:9]:
             copy.wait()
-        head_data = dot(normed, w_token_ref[...]).astype(BF)
-        tiles(head_data, mask_ref, qg_ref, kv_ref, device)
-
-    q_slot = lax.rem(a, group_q) * n_row + r
+        choose = chooser()
+
+    q_four = lax.rem(a, group_q)
+    q_slot = q_four * n_row + r
     k_four = lax.rem(a, group_k)
     k_slot = k_four * n_col + c
 
     def q_copy(to):
         return pltpu.make_async_remote_copy(
             src_ref=qg_ref.at[to],
-            dst_ref=qall_ref.at[q_slot, c],
+            dst_ref=qown_ref.at[q_four, r],
             send_sem=send.at[0, to],
             recv_sem=q_sem.at[q_slot],
             device_id=(to, a // group_q, c),
@@ -359,7 +351,7 @@
     def k_copy(to):
         return pltpu.make_async_remote_copy(
             src_ref=kv_ref.at[to],
-            dst_ref=kall_ref.at[r, k_four, c],
+            dst_ref=kown_ref.at[k_four, c],
             send_sem=send.at[1, to],
             recv_sem=k_sem.at[k_slot],
             device_id=(to, r, a // group_k),
@@ -374,59 +366,80 @@
 
         lax.fori_loop(0, n_atom, sent, 0)
 
-    def start(i, carry):
-        half = n_atom // 2
-        to = lax.rem(a // half + 1 + i // half, 2) * half + lax.rem(a + i, half)
-        unless(
-            own_k & (to == a),
-            lambda: k_copy(to).start(),
-            lambda: pltpu.make_async_copy(
-                kv_ref.at[to], kall_ref.at[r, k_four, c], k_sem.at[k_slot]
-            ).start(),
-        )
-        unless(
-            own_q & (to == a),
-            lambda: q_copy(to).start(),
-            lambda: pltpu.make_async_copy(
-                qg_ref.at[to], qall_ref.at[q_slot, c], q_sem.at[q_slot]
-            ).start(),
-        )
-        return carry
-
-    with jax.named_scope("send_tiles"):
-        lax.fori_loop(0, n_atom, start, 0)
+    half = n_atom // 2
+    columns = half * 4 * HD
+    for k in range(2):
+        first = lax.rem(a // half + 1 + k, 2) * half
+        with jax.named_scope("tiles"):
+            span = pl.ds(pl.multiple_of(first * 4 * HD, 128), columns)
+            head_data = dot(normed, w_token_ref[:, span]).astype(BF)
+            tiles(head_data, choose, first, qg_ref, kv_ref)
+
+        def start(i, carry):
+            to = first + lax.rem(a + i, half)
+            unless(
+                own_k & (to == a),
+                lambda: k_copy(to).start(),
+                lambda: pltpu.make_async_copy(
+                    kv_ref.at[to], kown_ref.at[k_four, c], k_sem.at[k_slot]
+                ).start(),
+            )
+            unless(
+                own_q & (to == a),
+                lambda: q_copy(to).start(),
+                lambda: pltpu.make_async_copy(
+                    qg_ref.at[to], qown_ref.at[q_four, r], q_sem.at[q_slot]
+                ).start(),
+            )
+            return carry
+
+        with jax.named_scope("send_tiles"):
+            lax.fori_loop(0, half, start, 0)
 
     def arrive_k(i, carry):
         pltpu.make_async_copy(
-            kv_ref.at[0], kall_ref.at[r, i // n_col, i % n_col], k_sem.at[i]
+            kv_ref.at[0], kown_ref.at[i // n_col, lax.rem(i, n_col)], k_sem.at[i]
         ).wait()
         return carry
 
     def arrive_q(i, carry):
-        pltpu.make_async_copy(qg_ref.at[0], qall_ref.at[i, c], q_sem.at[i]).wait()
+        pltpu.make_async_copy(
+            qg_ref.at[0], qown_ref.at[i // n_row, lax.rem(i, n_row)], q_sem.at[i]
+        ).wait()
         return carry
 
     def gather_q(step):
-        mine = qall_ref.at[:, c]
         return pltpu.make_async_remote_copy(
-            src_ref=mine,
-            dst_ref=mine,
+            src_ref=qpack_ref.at[c],
+            dst_ref=qpack_ref.at[c],
             send_sem=g_send.at[0, step],
             recv_sem=gq_sem.at[step],
             device_id=(a, r, lax.rem(c + step, n_col)),
             device_id_type=MESH,
         )
 
+    def gather_g(step):
+        to = lax.rem(c + step, n_col)
+        return pltpu.make_async_remote_copy(
+            src_ref=qown_ref.at[:, to],
+            dst_ref=gate_ref.at[:, c],
+            send_sem=g_send.at[2, step],
+            recv_sem=gg_sem.at[step],
+            device_id=(a, r, to),
+            device_id_type=MESH,
+        )
+
     def partner(step):
         half = n_row // 2
         return lax.rem(r // 2 + step // 2, half) * 2 + lax.rem(lax.rem(r, 2) + step % 2, 2)
 
-    def gather_k(step):
+    def gather_k(step, value):
+        mine = keys_ref.at[r, pl.ds(LAST if value else 0, HD)]
         return pltpu.make_async_remote_copy(
-            src_ref=kall_ref.at[r],
-            dst_ref=kall_ref.at[r],
-            send_sem=g_send.at[1, step],
-            recv_sem=gk_sem.at[step],
+            src_ref=mine,
+            dst_ref=mine,
+            send_sem=g_send.at[3 + value, step],
+            recv_sem=gk_sem.at[value, step],
             device_id=(a, partner(step), c),
             device_id_type=MESH,
         )
@@ -434,29 +447,54 @@
     def drain_gather():
         for step in range(1, n_col):
             gather_q(step).wait_send()
+            gather_g(step).wait_send()
         for step in range(1, n_row):
-            gather_k(step).wait_send()
-
-    with jax.named_scope("tiles_arrive"):
-        lax.fori_loop(0, n_atom, arrive_q, 0)
-        for step in range(1, n_col):
-            gather_q(step).start()
-        lax.fori_loop(0, n_atom, arrive_k, 0)
-        for step in range(1, n_row):
-            gather_k(step).start()
-    for copy in loads[9:]:
-        copy.wait()
-    with jax.named_scope("gather_q"):
-        for step in range(1, n_col):
-            gather_q(step).wait_recv()
+            gather_k(step, 0).wait_send()
+            gather_k(step, 1).wait_send()
+
     q_rows, keys = pair_ref.shape[1:]
     per_slot = q_rows // n_atom
     per_row = keys // n_row
-    lane = iota((q_rows, 128), 1)
-    queries = qall_ref[...].reshape(q_rows, 128)
-    query_ref[...] = jnp.where(
-        (lane >= HD) & (lane <= 2 * HD), queries, jnp.zeros_like(queries)
-    )
+    live = jnp.sum(jnp.sum(mask_ref[...], axis=0, keepdims=True), axis=1, keepdims=True)
+    kind, column = iota((32, per_row), 0), iota((32, per_row), 1)
+    token = (group_k * c + column // per_slot) * per_row + lax.rem(column, per_slot)
+    for i in range(n_row):
+        masked = jnp.where(token + i * per_slot < live, 0.0, NEG)
+        extra = jnp.where(kind == 0, masked, jnp.where(kind == 1, 1.0, 0.0))
+        keys_ref[i, HD:LAST] = extra.astype(BF)
+    with jax.named_scope("tiles_arrive"):
+        lax.fori_loop(0, n_atom, arrive_k, 0)
+        moved = jnp.transpose(kown_ref[...].reshape(per_row, 128).astype(F32))
+        keys_ref[r, :HD] = moved[:HD].astype(BF)
+        keys_ref[r, LAST:] = moved[LAST:].astype(BF)
+        for value in range(2):
+            for step in range(1, n_row):
+                gather_k(step, value).start()
+        lax.fori_loop(0, n_atom, arrive_q, 0)
+        half = q_rows // n_col // 2
+        lane = iota((half, 128), 1)
+        low = qown_ref[: group_q // 2].reshape(half, 128).astype(F32)
+        high = qown_ref[group_q // 2 :].reshape(half, 128).astype(F32)
+        qpack_ref[c] = jnp.where(lane < 64, low, pltpu.roll(high, 64, 1)).astype(BF)
+        for step in (2, 1, 3):
+            gather_q(step).start()
+        for step in range(1, n_col):
+            gather_g(step).start()
+        gate_ref[:, c] = qown_ref[:, c]
+    with jax.named_scope("gather_q"):
+        wanted = lane < HD
+        one = jnp.where(lane == HD, 1.0, 0.0)
+        for step in range(n_col):
+            source = lax.rem(c + n_col - step, n_col)
+            if step > 0:
+                gather_q(step).wait_recv()
+            packed = qpack_ref[source].astype(F32)
+            for i, value in enumerate((packed, pltpu.roll(packed, 64, 1))):
+                value = jnp.where(wanted, value, one).astype(BF)
+                slots = slice(n_atom // 2 * i, n_atom // 2 * (i + 1))
+                query_ref[slots, source] = value.reshape(n_atom // 2, half * 2 // n_atom, 128)
+    for copy in loads[9:]:
+        copy.wait()
     peak_ref[...] = jnp.full_like(peak_ref, -jnp.inf)
 
     def score(step, carry):
@@ -464,10 +502,9 @@
 
         @pl.when(step > 0)
         def _():
-            mine = kall_ref.at[source]
-            pltpu.make_async_copy(mine, mine, gk_sem.at[step]).wait()
-
-        held = kall_ref[source].reshape(per_row, 128)
+            mine = keys_ref.at[source, pl.ds(0, HD)]
+            pltpu.make_async_copy(mine, mine, gk_sem.at[0, step]).wait()
+
         half = q_rows // 2
         span = half // (n_row * per_slot)
         for i in range(2):
@@ -475,8 +512,9 @@
             fours = slice(span * i, span * (i + 1))
             peak = peak_ref[fours]
             for at in range(0, per_row, 256):
-                part = lax.dot_general(
-                    query_ref[rows], held[at : at + 256], NT, preferred_element_type=F32
+                part = dot(
+                    query_ref[n_atom // 2 * i : n_atom // 2 * (i + 1)].reshape(half, 128)[:, :LAST],
+                    keys_ref[source, :LAST, at : at + 256],
                 )
                 for k in range(0, 256, 128):
                     four = (at + k) // 128
@@ -509,7 +547,9 @@
             partial(step).wait_send()
 
     def quarter(i, carry):
-        to = lax.rem(c + i + 1, n_col)
+        late = i // 2
+        step = (1 - late) * (2 - i) + late * (i + 1)
+        to = lax.rem(c + step, n_col)
         results = []
         for h in range(2):
             fours = slice(2 * h, 2 * h + 2)
@@ -517,21 +557,33 @@
             for at in range(0, keys, 256):
                 part = score_ref[fours, to, :, at : at + 256].reshape(2 * per_slot, 256)
                 weight_ref[h, :, at : at + 256] = jnp.exp(part - top).astype(BF)
-            mixed = dot(weight_ref[h], kall_ref[...].reshape(keys, 128))
+            mixed = sum(
+                lax.dot_general(
+                    weight_ref[h, :, per_row * k : per_row * (k + 1)],
+                    keys_ref[k],
+                    NT,
+                    preferred_element_type=F32,
+                )
+                for k in range(n_row)
+            )
             results.append(summary(mixed, top))
         part_ref[to] = paired(*results).astype(BF)
 
         @pl.when(i < n_col - 1)
         def _():
-            partial(i + 1).start()
+            partial(step).start()
 
         return carry
 
+    with jax.named_scope("values_arrive"):
+        for step in range(1, n_row):
+            gather_k(step, 1).wait_recv()
     with jax.named_scope("attention"):
         lax.fori_loop(0, n_col, quarter, 0)
     with jax.named_scope("partials_arrive"):
         for step in range(1, n_col):
             partial(step).wait_recv()
+            gather_g(step).wait_recv()
 
     def head_copy(j, k):
         return pltpu.make_async_remote_copy(
@@ -572,13 +624,13 @@
         parts = [part_ref[c]] + [got_ref[step] for step in range(1, n_col)]
         gates = [
             jnp.concatenate(
-                [qall_ref[n_row * u + c].reshape(per_slot, 128) for u in (2 * h, 2 * h + 1)], axis=0
+                [gate_ref[u].reshape(per_slot, 128) for u in (2 * h, 2 * h + 1)], axis=0
             ).astype(F32)
             for h in range(2)
         ]
         attended = merged(parts, paired(*gates))
         for u in range(group_k):
-            at = 64 * (u // 2)
+            at = LAST - 64 * (u // 2)
             head_ref[u] = attended[at : at + HD, out_rows * (u % 2) : out_rows * (u % 2 + 1)]
     with jax.named_scope("send_heads"):
         lax.fori_loop(0, group_k, one_head, 0)
@@ -598,6 +650,12 @@
     drain_gather()
     drain_partials()
     drain_heads()
+
+
+def split_kernel(both_ref, update_ref, out_ref):
+    rows = update_ref.shape[0]
+    update_ref[...] = both_ref[:rows]
+    out_ref[...] = both_ref[rows:]
 
 
 def shards(
@@ -648,9 +706,12 @@
             pltpu.VMEM((rows, width), F32),
             pltpu.VMEM((n_atom, toks, 128), BF),
             pltpu.VMEM((n_atom, toks, 128), BF),
+            pltpu.VMEM((n_atom // n_row, n_row, toks, 128), BF),
+            pltpu.VMEM((group, n_col, toks, 128), BF),
+            pltpu.VMEM((n_col, tile_rows, 128), BF),
+            pltpu.VMEM((group, n_col, toks, 128), BF),
+            pltpu.VMEM((n_row, 128, k_cols // n_row), BF),
             pltpu.VMEM((n_atom, n_col, toks, 128), BF),
-            pltpu.VMEM((n_row, group, n_col, toks, 128), BF),
-            pltpu.VMEM((q_rows, 128), BF),
             pltpu.VMEM((group, n_row, out_rows, 128), F32),
             pltpu.VMEM((group, n_row, out_rows, k_cols), F32),
             pltpu.VMEM((2, tile_rows, k_cols), BF),
@@ -664,9 +725,10 @@
             dma((2, n_atom)),
             dma((n_atom,)),
             dma((n_atom,)),
-            dma((2, max(n_row, n_col))),
+            dma((5, max(n_row, n_col))),
             dma((n_col,)),
-            dma((n_row,)),
+            dma((2, n_row)),
+            dma((n_col,)),
             dma((n_col,)),
             dma((n_col,)),
             dma((group, n_col)),
@@ -676,7 +738,16 @@
             collective_id=0, has_side_effects=True, vmem_limit_bytes=56 << 20
         ),
     )(window_start, *operands)
-    return (both[:rows], both[rows:].T)
+    update, flipped = pl.pallas_call(
+        split_kernel,
+        out_shape=(
+            jax.ShapeDtypeStruct((rows, width), BF),
+            jax.ShapeDtypeStruct((w_out.shape[1], out_rows), BF),
+        ),
+        in_specs=[VMEM],
+        out_specs=(VMEM, VMEM),
+    )(both)
+    return (update, flipped.T)
 
 
 def solution(mesh):

time: 65.8 us -> 60.9 us (0.926)
  local copies, waits for them, and re-layouts: 2.89 us -> 0 us
  Pallas kernels: 62.1 us -> 60.1 us
    pallas_call x1, Pallas kernels: 62.1 us -> 58.6 us  [shards(): pl.pallas_call(functools.partial(whole_kernel, rows * devices), out_shape...]
    pallas_call x0 -> x1, Pallas kernels: none -> 1.55 us  [shards(): pl.pallas_call(split_kernel, out_shape=(jax.ShapeDtypeStruct((rows, width...]
    slice x1 -> x0, local copies, waits for them, and re-layouts: 1.47 us -> none  [shards(): return (both[:rows], both[rows:].T)]
    transpose x1 -> x0, local copies, waits for them, and re-layouts: 1.42 us -> none  [shards(): return (both[:rows], both[rows:].T)]
where the time goes in v2:
time: 60.9 us; the launch traced here: 60.8 us
  Pallas kernels  60.1 us (99%)
  between operations  0.64 us (1%)
    pallas_call x1, Pallas kernels, shards(): pl.pallas_call(functools.partial(whole_kernel, rows * devices), out_shape...  58.6 us
    pallas_call x1, Pallas kernels, shards(): pl.pallas_call(split_kernel, out_shape=(jax.ShapeDtypeStruct((rows, width...  1.55 us

profile of v2, /device:TPU:1, one launch (start us, length us, event | category | flops | bytes accessed | tf_op | source)
XLA Modules:
  0.0 60.8 jit_solution(17732503546389954056)
XLA Ops:
  0.6 58.6 %shard_map.131.both_ref = bf16[448,128]{1,0:T(8,128)(2,1)} custom-call(s32[8]{0:T(128)} %start_ref.1, bf16[256,128]{1,0:T(8,128)(2,1)} %feats_in.1, bf16[128,512]{1,0:T(8,128)(2,1)} %w_atom_in.1, bf16[256,512]{1,0:T(8,128)(2,1)} %bias_in.1, bf16[128,128]{1,0:T(8,128)(2,1)} %w_atom_out_in.1, bf16[128,768]{1,0:T(8,128)(2,1)} %w_to_token_in.1, ...), custom_call_target="tpu_custom_call" | custom-call | tf_op jit(solution)/shard_map/pallas_call | solution.py:698
  59.2 1.5 %shard_map.132 = (bf16[256,128]{1,0:T(8,128)(2,1)}, bf16[192,128]{1,0:T(8,128)(2,1)}) custom-call(bf16[448,128]{1,0:T(8,128)(2,1)} %shard_map.131.both_ref), custom_call_target="tpu_custom_call" | custom-call | tf_op jit(solution)/shard_map/pallas_call | solution.py:741

commit v3 on v2

--- a/solution.py
+++ b/solution.py
@@ -39,10 +39,6 @@
 
 def place():
     return lax.axis_index("atom"), lax.axis_index("row"), lax.axis_index("col")
-
-
-def project(feats, w_atom_ref, first, last):
-    return dot(layer_norm(feats.astype(F32)), w_atom_ref[:, first:last])
 
 
 def window(b, all_atoms, first_atom, start, query, pairs, bias_ref):
@@ -175,6 +171,7 @@
     mask_ref,
     pair_ref,
     w_out_ref,
+    edge_ref,
     halo_ref,
     mixed_ref,
     qg_ref,
@@ -243,7 +240,7 @@
     own_h = lax.rem(a, n_row) == c
 
     def greet(i, carry):
-        signal((i, r, lax.rem(a, n_row)))
+        signal((lax.rem(i + n_atom // 2 * (1 - a // (n_atom // 2)), n_atom), r, lax.rem(a, n_row)))
         signal((group_k * c + i // n_col, r, lax.rem(i, n_col)))
         signal((group_q * r + i // n_row, lax.rem(i, n_row), c))
         return carry
@@ -259,9 +256,8 @@
 
     def halo_copy(side):
         other = lax.rem(device + (1 if side == 0 else devices - 1), devices)
-        edge = rows - HALO if side == 0 else 0
         return pltpu.make_async_remote_copy(
-            src_ref=feats_in.at[pl.ds(edge, HALO)],
+            src_ref=edge_ref.at[side],
             dst_ref=halo_ref.at[side],
             send_sem=halo_send.at[side],
             recv_sem=halo_recv.at[side],
@@ -285,9 +281,11 @@
     first_atom = device * rows
     with jax.named_scope("inner_windows"):
         feats = feats_ref[...]
-        proj = project(feats, w_atom_ref, 0, 4 * width)
+        proj = dot(layer_norm(feats.astype(F32)), w_atom_ref[...])
         queries = proj[:, :width].astype(BF)
         pairs = proj[:, width : 3 * width].astype(BF)
+        edge_ref[0] = pairs[rows - HALO :]
+        edge_ref[1] = pairs[:HALO]
         gate = jax.nn.sigmoid(proj[:, 3 * width :])
         edge = HALO // QB
         blocks = rows // QB
@@ -311,9 +309,7 @@
         for side in range(2):
             halo_copy(side).wait_recv()
     with jax.named_scope("outer_windows"):
-        around = project(halo_ref[...].reshape(2 * HALO, width), w_atom_ref, width, 3 * width)
-        around = around.astype(BF)
-        before, after = around[:HALO], around[HALO:]
+        before, after = halo_ref[0], halo_ref[1]
         wide = jnp.concatenate([before, pairs[: QB * 2 * edge]], axis=0)
         for b in range(edge):
             one_window(b, wide[QB * b : QB * (b + 2 * edge + 1)])
@@ -378,17 +374,17 @@
         def start(i, carry):
             to = first + lax.rem(a + i, half)
             unless(
+                own_q & (to == a),
+                lambda: q_copy(to).start(),
+                lambda: pltpu.make_async_copy(
+                    qg_ref.at[to], qown_ref.at[q_four, r], q_sem.at[q_slot]
+                ).start(),
+            )
+            unless(
                 own_k & (to == a),
                 lambda: k_copy(to).start(),
                 lambda: pltpu.make_async_copy(
                     kv_ref.at[to], kown_ref.at[k_four, c], k_sem.at[k_slot]
-                ).start(),
-            )
-            unless(
-                own_q & (to == a),
-                lambda: q_copy(to).start(),
-                lambda: pltpu.make_async_copy(
-                    qg_ref.at[to], qown_ref.at[q_four, r], q_sem.at[q_slot]
                 ).start(),
             )
             return carry
@@ -610,8 +606,9 @@
 
     out_rows = head_ref.shape[2]
 
-    def one_head(j, carry):
-        for k in range(1, n_col):
+    def one_head(i, carry):
+        j = lax.rem(i + group_k // 2 * (1 - a // (n_atom // 2)), group_k)
+        for k in (2, 1, 3):
             head_copy(j, k).start()
         unless(
             own_h & (n_row * j + c == a),
@@ -702,7 +699,8 @@
         out_specs=VMEM,
         scratch_shapes=[pltpu.VMEM(x.shape, x.dtype) for x in operands]
         + [
-            pltpu.VMEM((2, HALO, width), BF),
+            pltpu.VMEM((2, HALO, 2 * width), BF),
+            pltpu.VMEM((2, HALO, 2 * width), BF),
             pltpu.VMEM((rows, width), F32),
             pltpu.VMEM((n_atom, toks, 128), BF),
             pltpu.VMEM((n_atom, toks, 128), BF),

time: 60.9 us -> 60.9 us (level)
  no operation moved by 1% of the time
where the time goes in v3:
time: 60.9 us; the launch traced here: 60.8 us
  Pallas kernels  60.2 us (99%)
  between operations  0.64 us (1%)
    pallas_call x1, Pallas kernels, shards(): pl.pallas_call(functools.partial(whole_kernel, rows * devices), out_shape...  58.6 us
    pallas_call x1, Pallas kernels, shards(): pl.pallas_call(split_kernel, out_shape=(jax.ShapeDtypeStruct((rows, width...  1.55 us

profile of v3, /device:TPU:1, one launch (start us, length us, event | category | flops | bytes accessed | tf_op | source)
XLA Modules:
  0.0 60.8 jit_solution(16330179628337768887)
XLA Ops:
  0.6 58.6 %shard_map.131.both_ref = bf16[448,128]{1,0:T(8,128)(2,1)} custom-call(s32[8]{0:T(128)} %start_ref.1, bf16[256,128]{1,0:T(8,128)(2,1)} %feats_in.1, bf16[128,512]{1,0:T(8,128)(2,1)} %w_atom_in.1, bf16[256,512]{1,0:T(8,128)(2,1)} %bias_in.1, bf16[128,128]{1,0:T(8,128)(2,1)} %w_atom_out_in.1, bf16[128,768]{1,0:T(8,128)(2,1)} %w_to_token_in.1, ...), custom_call_target="tpu_custom_call" | custom-call | tf_op jit(solution)/shard_map/pallas_call | solution.py:695
  59.3 1.5 %shard_map.132 = (bf16[256,128]{1,0:T(8,128)(2,1)}, bf16[192,128]{1,0:T(8,128)(2,1)}) custom-call(bf16[448,128]{1,0:T(8,128)(2,1)} %shard_map.131.both_ref), custom_call_target="tpu_custom_call" | custom-call | tf_op jit(solution)/shard_map/pallas_call | solution.py:739

commit v4 on v2

--- a/solution.py
+++ b/solution.py
@@ -550,23 +550,28 @@
         late = i // 2
         step = (1 - late) * (2 - i) + late * (i + 1)
         to = lax.rem(c + step, n_col)
-        results = []
-        for h in range(2):
-            fours = slice(2 * h, 2 * h + 2)
-            top = jnp.max(peak_ref[fours, to].reshape(2 * per_slot, 128), axis=1, keepdims=True)
-            for at in range(0, keys, 256):
-                part = score_ref[fours, to, :, at : at + 256].reshape(2 * per_slot, 256)
-                weight_ref[h, :, at : at + 256] = jnp.exp(part - top).astype(BF)
-            mixed = sum(
-                lax.dot_general(
-                    weight_ref[h, :, per_row * k : per_row * (k + 1)],
-                    keys_ref[k],
-                    NT,
-                    preferred_element_type=F32,
-                )
-                for k in range(n_row)
+        tops = [
+            jnp.max(peak_ref[2 * h : 2 * h + 2, to].reshape(2 * per_slot, 128), axis=1, keepdims=True)
+            for h in range(2)
+        ]
+        mixed = None
+        for k in range(n_row):
+            for h in range(2):
+                for at in range(per_row * k, per_row * (k + 1), 256):
+                    part = score_ref[2 * h : 2 * h + 2, to, :, at : at + 256]
+                    part = jnp.exp(part.reshape(2 * per_slot, 256) - tops[h])
+                    weight_ref[h, :, at : at + 256] = part.astype(BF)
+            weights = weight_ref[:, :, per_row * k : per_row * (k + 1)]
+            piece = lax.dot_general(
+                weights.reshape(4 * per_slot, per_row),
+                keys_ref[k],
+                NT,
+                preferred_element_type=F32,
             )
-            results.append(summary(mixed, top))
+            mixed = piece if mixed is None else mixed + piece
+        results = [
+            summary(mixed[2 * per_slot * h : 2 * per_slot * (h + 1)], tops[h]) for h in range(2)
+        ]
         part_ref[to] = paired(*results).astype(BF)
 
         @pl.when(i < n_col - 1)

time: 60.9 us -> 60.9 us (level)
  no operation moved by 1% of the time
where the time goes in v4:
time: 60.9 us; the launch traced here: 60.7 us
  Pallas kernels  60.1 us (99%)
  between operations  0.64 us (1%)
    pallas_call x1, Pallas kernels, shards(): pl.pallas_call(functools.partial(whole_kernel, rows * devices), out_shape...  58.5 us
    pallas_call x1, Pallas kernels, shards(): pl.pallas_call(split_kernel, out_shape=(jax.ShapeDtypeStruct((rows, width...  1.55 us

profile of v4, /device:TPU:1, one launch (start us, length us, event | category | flops | bytes accessed | tf_op | source)
XLA Modules:
  0.0 60.7 jit_solution(7724655507090108667)
XLA Ops:
  0.6 58.5 %shard_map.131.both_ref = bf16[448,128]{1,0:T(8,128)(2,1)} custom-call(s32[8]{0:T(128)} %start_ref.1, bf16[256,128]{1,0:T(8,128)(2,1)} %feats_in.1, bf16[128,512]{1,0:T(8,128)(2,1)} %w_atom_in.1, bf16[256,512]{1,0:T(8,128)(2,1)} %bias_in.1, bf16[128,128]{1,0:T(8,128)(2,1)} %w_atom_out_in.1, bf16[128,768]{1,0:T(8,128)(2,1)} %w_to_token_in.1, ...), custom_call_target="tpu_custom_call" | custom-call | tf_op jit(solution)/shard_map/pallas_call | solution.py:703
  59.2 1.5 %shard_map.132 = (bf16[256,128]{1,0:T(8,128)(2,1)}, bf16[192,128]{1,0:T(8,128)(2,1)}) custom-call(bf16[448,128]{1,0:T(8,128)(2,1)} %shard_map.131.both_ref), custom_call_target="tpu_custom_call" | custom-call | tf_op jit(solution)/shard_map/pallas_call | solution.py:746

commit v5 on v3

--- a/solution.py
+++ b/solution.py
@@ -546,23 +546,28 @@
         late = i // 2
         step = (1 - late) * (2 - i) + late * (i + 1)
         to = lax.rem(c + step, n_col)
-        results = []
-        for h in range(2):
-            fours = slice(2 * h, 2 * h + 2)
-            top = jnp.max(peak_ref[fours, to].reshape(2 * per_slot, 128), axis=1, keepdims=True)
-            for at in range(0, keys, 256):
-                part = score_ref[fours, to, :, at : at + 256].reshape(2 * per_slot, 256)
-                weight_ref[h, :, at : at + 256] = jnp.exp(part - top).astype(BF)
-            mixed = sum(
-                lax.dot_general(
-                    weight_ref[h, :, per_row * k : per_row * (k + 1)],
-                    keys_ref[k],
-                    NT,
-                    preferred_element_type=F32,
-                )
-                for k in range(n_row)
+        tops = [
+            jnp.max(peak_ref[2 * h : 2 * h + 2, to].reshape(2 * per_slot, 128), axis=1, keepdims=True)
+            for h in range(2)
+        ]
+        mixed = None
+        for k in range(n_row):
+            for h in range(2):
+                for at in range(per_row * k, per_row * (k + 1), 256):
+                    part = score_ref[2 * h : 2 * h + 2, to, :, at : at + 256]
+                    part = jnp.exp(part.reshape(2 * per_slot, 256) - tops[h])
+                    weight_ref[h, :, at : at + 256] = part.astype(BF)
+            weights = weight_ref[:, :, per_row * k : per_row * (k + 1)]
+            piece = lax.dot_general(
+                weights.reshape(4 * per_slot, per_row),
+                keys_ref[k],
+                NT,
+                preferred_element_type=F32,
             )
-            results.append(summary(mixed, top))
+            mixed = piece if mixed is None else mixed + piece
+        results = [
+            summary(mixed[2 * per_slot * h : 2 * per_slot * (h + 1)], tops[h]) for h in range(2)
+        ]
         part_ref[to] = paired(*results).astype(BF)
 
         @pl.when(i < n_col - 1)

time: 60.9 us -> 60.9 us (level)
  no operation moved by 1% of the time
where the time goes in v5:
time: 60.9 us; the launch traced here: 60.8 us
  Pallas kernels  60.2 us (99%)
  between operations  0.64 us (1%)
    pallas_call x1, Pallas kernels, shards(): pl.pallas_call(functools.partial(whole_kernel, rows * devices), out_shape...  58.6 us
    pallas_call x1, Pallas kernels, shards(): pl.pallas_call(split_kernel, out_shape=(jax.ShapeDtypeStruct((rows, width...  1.55 us

profile of v5, /device:TPU:1, one launch (start us, length us, event | category | flops | bytes accessed | tf_op | source)
XLA Modules:
  0.0 60.8 jit_solution(11938564292466623206)
XLA Ops:
  0.6 58.6 %shard_map.131.both_ref = bf16[448,128]{1,0:T(8,128)(2,1)} custom-call(s32[8]{0:T(128)} %start_ref.1, bf16[256,128]{1,0:T(8,128)(2,1)} %feats_in.1, bf16[128,512]{1,0:T(8,128)(2,1)} %w_atom_in.1, bf16[256,512]{1,0:T(8,128)(2,1)} %bias_in.1, bf16[128,128]{1,0:T(8,128)(2,1)} %w_atom_out_in.1, bf16[128,768]{1,0:T(8,128)(2,1)} %w_to_token_in.1, ...), custom_call_target="tpu_custom_call" | custom-call | tf_op jit(solution)/shard_map/pallas_call | solution.py:700
  59.3 1.5 %shard_map.132 = (bf16[256,128]{1,0:T(8,128)(2,1)}, bf16[192,128]{1,0:T(8,128)(2,1)}) custom-call(bf16[448,128]{1,0:T(8,128)(2,1)} %shard_map.131.both_ref), custom_call_target="tpu_custom_call" | custom-call | tf_op jit(solution)/shard_map/pallas_call | solution.py:744
